TPU v7x, 32 devices: a whole 2x2x4 slice. The times are simulated.
32 devices in a mesh: tile: 2 (over y), gz: 4 (over z), gy: 2 (over x), view: 2 (over core).
Axes of the slice: x: 2, y: 2, z: 4, core: 2. Of those that a mesh axis runs over, the one named last changes fastest.
Arguments:
- images: float32 [6, 128, 128, 128], P('view', ('tile', 'gz'), 'gy'), parts along dimension 1, may hold values from 0.3 to 3
- estimate: float32 [128, 128, 128], P(('tile', 'gz'), 'gy'), parts along dimension 0, may hold values from 0.5 to 2
- psf: float32 [6, 3, 31], P('view'), may hold values from 0.05 to 1
- coverage: int32 [6, 8, 2], P('view', ('tile', 'gz'), 'gy'), parts along dimension 1, may hold values from 0 to 1
Outputs:
- deconvolved: float32 [128, 128, 128], P(('tile', 'gz'), 'gy'), parts along dimension 0
There are 2 independent parts, one for each index of `tile`. A program takes and returns all parts, laid end to end along the dimension named above; an argument that names none is the same for every part. Nothing has to cross between parts.
All inputs are finite; a program needn't handle non-finite values.
Results may differ from a plain program's by a relative error of at most 0.0001.
Values sent between devices are 32-bit elements; how exact they have to be, the bound alone decides.
A program may use at most 64 MiB of HBM per device.

v0:
```python
import jax
import jax.numpy as jnp
from jax import lax
from jax.sharding import PartitionSpec as P

HALF = 15


def padded_2(x, sides, width):
    for axis, dim in sides:
        peers, length = (lax.axis_size(axis), x.shape[dim])
        up = [(i, (i + 1) % peers) for i in range(peers - 1)]
        down = [(j, i) for i, j in up]
        last = lax.slice_in_dim(x, length - width, length, axis=dim)
        first = lax.slice_in_dim(x, 0, width, axis=dim)
        before = lax.ppermute(last, axis, up)
        after = lax.ppermute(first, axis, down)
        x = jnp.concatenate([before, x, after], axis=dim)
    return x


def joined(value, axis, join):
    pieces = lax.all_gather(value, axis)
    head = pieces[0]
    tail = pieces[1:]
    running, _ = lax.scan(lambda running, slab: (join(running, slab), None), head, tail)
    return running


def band_matrix(kernels, length):
    rows = jnp.arange(length)[:, None]
    cols = jnp.arange(length + 2 * HALF)[None, :]
    offset = cols - rows
    onehot = (offset[:, :, None] == jnp.arange(2 * HALF + 1)[None, None, :]).astype(jnp.float32)
    return jnp.einsum("ijk,vk->vij", onehot, kernels, precision=lax.Precision.HIGHEST)


def tile_width():
    return 128


def x_pass(along_y, x_band):
    padded = jnp.pad(along_y, ((0, 0), (0, 0), (0, 0), (HALF, HALF)))
    pieces = [padded]
    stacked = jnp.stack(pieces, axis=3)
    result = jnp.einsum("vzytj,vij->vzyti", stacked, x_band, precision=lax.Precision.HIGHEST)
    return result.reshape(along_y.shape)


def finish_blur(along_z, y_band, x_band):
    along_y = jnp.einsum("vij,vzjx->vzix", y_band, along_z, precision=lax.Precision.HIGHEST)
    return x_pass(along_y, x_band)


def multiply(first, second):
    return first * second


def body(images, estimate, psf, coverage):
    kernel = psf / jnp.sum(psf, axis=2, keepdims=True)
    flipped = kernel[:, :, ::-1]
    depth, height, width = estimate.shape
    span = tile_width()
    fwd_z = band_matrix(kernel[:, 0], depth)
    fwd_y = band_matrix(kernel[:, 1], height)
    fwd_x = band_matrix(kernel[:, 2], span)
    back_z = band_matrix(flipped[:, 0], depth)
    back_y = band_matrix(flipped[:, 1], height)
    back_x = band_matrix(flipped[:, 2], span)
    covered = coverage[:, 0, 0] > 0
    field = estimate
    padded = padded_2(field, (("gz", 0), ("gy", 1)), HALF)
    along_z = jnp.einsum("vij,jyx->viyx", fwd_z, padded, precision=lax.Precision.HIGHEST)
    blurred = finish_blur(along_z, fwd_y, fwd_x)
    ratio = images / blurred
    ratio_pad = padded_2(ratio, (("gz", 1), ("gy", 2)), HALF)
    back_along = jnp.einsum("vij,vjyx->viyx", back_z, ratio_pad, precision=lax.Precision.HIGHEST)
    correction = finish_blur(back_along, back_y, back_x)
    masked = jnp.where(covered[:, None, None, None], correction, jnp.float32(1.0))
    local_product = jnp.prod(masked, axis=0)
    factor = joined(local_product, "view", multiply)
    field = field * factor
    return field


def solution(mesh):
    return jax.shard_map(
        body,
        mesh=mesh,
        in_specs=(
            P("view", ("tile", "gz"), "gy", None),
            P(("tile", "gz"), "gy", None),
            P("view", None, None),
            P("view", ("tile", "gz"), "gy"),
        ),
        out_specs=P(("tile", "gz"), "gy", None),
        check_vma=False,
    )
```

profile of v0, /device:TPU:0, one launch (start us, length us, event | category | flops | bytes accessed | tf_op | source)
XLA Modules:
  0.0 150.2 jit_solution(15454627238384890405)
XLA Ops:
  6.5 1.4 copy.5
  8.0 5.0 %collective-permute-start = (f32[15,64,128]{2,0,1:T(8,128)S(1)}, f32[15,64,128]{2,0,1:T(8,128)S(1)}, u32[]{:S(2)}, u32[]{:S(2)}) collective-permute-start(f32[15,64,128]{2,0,1:T(8,128)S(1)} %get-tuple-element.20), channel_id=1, source_target_pairs={{0,4},{4,8},{8,12},{1,5},{5,9},{9,13},{2,6},{6,10},{10,14},{3,7},{... | collective-permute-start | bytes 1474568 | tf_op jit(solution)/shard_map/ppermute | solution.py:16
  12.9 1.3 collective-permute-start.1
  14.7 9.4 %collective-permute-done = f32[15,64,128]{2,0,1:T(8,128)S(1)} collective-permute-done((f32[15,64,128]{2,0,1:T(8,128)S(1)}, f32[15,64,128]{2,0,1:T(8,128)S(1)}, u32[]{:S(2)}, u32[]{:S(2)}) %collective-permute-start) | collective-permute-done | bytes 491552 | tf_op jit(solution)/shard_map/ppermute | solution.py:16
  24.1 4.1 %collective-permute-done.1 = f32[15,64,128]{2,0,1:T(8,128)S(1)} collective-permute-done((f32[15,64,128]{2,0,1:T(8,128)S(1)}, f32[15,64,128]{2,0,1:T(8,128)S(1)}, u32[]{:S(2)}, u32[]{:S(2)}) %collective-permute-start.1) | collective-permute-done | bytes 491552 | tf_op jit(solution)/shard_map/ppermute | solution.py:17
  28.3 3.4 %collective-permute-start.2 = (f32[46,15,128]{2,0,1:T(8,128)S(1)}, f32[46,15,128]{2,0,1:T(8,128)S(1)}, u32[]{:S(2)}, u32[]{:S(2)}) collective-permute-start(f32[46,15,128]{2,0,1:T(8,128)S(1)} %get-tuple-element.18), channel_id=1, source_target_pairs={{0,2},{1,3},{4,6},{5,7},{8,10},{9,11},{12,14},{13,15},{16,18},{17,... | collective-permute-start | bytes 1059848 | tf_op jit(solution)/shard_map/ppermute | solution.py:16
  31.7 1.3 collective-permute-start.3
  33.5 0.9 fusion.34
  34.4 4.0 %collective-permute-done.2 = f32[46,15,128]{2,0,1:T(8,128)S(1)} collective-permute-done((f32[46,15,128]{2,0,1:T(8,128)S(1)}, f32[46,15,128]{2,0,1:T(8,128)S(1)}, u32[]{:S(2)}, u32[]{:S(2)}) %collective-permute-start.2) | collective-permute-done | bytes 353312 | tf_op jit(solution)/shard_map/ppermute | solution.py:16
  38.3 4.1 %collective-permute-done.3 = f32[46,15,128]{2,0,1:T(8,128)S(1)} collective-permute-done((f32[46,15,128]{2,0,1:T(8,128)S(1)}, f32[46,15,128]{2,0,1:T(8,128)S(1)}, u32[]{:S(2)}, u32[]{:S(2)}) %collective-permute-start.3) | collective-permute-done | bytes 353312 | tf_op jit(solution)/shard_map/ppermute | solution.py:17
  42.5 2.0 %fusion.12 = f32[3,16,94,128]{3,1,2,0:T(8,128)S(1)} fusion(f32[46,15,128]{2,0,1:T(8,128)S(1)} %collective-permute-done.3, f32[15,64,128]{2,0,1:T(8,128)S(1)} %collective-permute-done.1, f32[16,64,128]{2,0,1:T(8,128)S(1)} %copy.5, f32[15,64,128]{2,0,1:T(8,128)S(1)} %collective-permute-done, f32[46,15,128]{2,0,1:T(8,128)S(1)} %collective-permute-done.2, ...), kind=kOutput, calls=%fused_computation.15 | convolution fusion | flops 321013760 | bytes 4532864 | tf_op jit(solution)/shard_map/vij,jyx->viyx/dot_general | solution.py:73
  44.6 2.4 %fusion.21 = f32[3,16,64,128]{3,2,1,0:T(8,128)S(1)} fusion(f32[3,16,94,128]{3,1,2,0:T(8,128)S(1)} %fusion.12, f32[3,64,94,1]{2,0,1,3:T(4,128)S(1)} %convolution_bitcast_fusion.1), kind=kOutput, calls=%fused_computation.25 | convolution fusion | flops 443547648 | bytes 3955200 | tf_op jit(solution)/shard_map/vij,vzjx->vzix/dot_general | solution.py:51
  47.0 3.0 %fusion.29 = f32[3,16,64,128]{3,2,1,0:T(8,128)S(1)} fusion(f32[3,16,64,128]{3,2,1,0:T(8,128)S(1)} %copy-done.4, f32[3,16,64,128]{3,2,1,0:T(8,128)S(1)} %fusion.21, f32[3,128,158,1]{1,0,2,3:T(4,128)S(1)} %fusion.34), kind=kOutput, calls=%fused_computation.27 | convolution fusion | flops 745930752 | bytes 4961280 | tf_op jit(solution)/shard_map/vzytj,vij->vzyti/dot_general | solution.py:46
  50.3 3.5 %collective-permute-start.4 = (f32[3,15,64,128]{3,2,1,0:T(8,128)S(1)}, f32[3,15,64,128]{3,2,1,0:T(8,128)S(1)}, u32[]{:S(2)}, u32[]{:S(2)}) collective-permute-start(f32[3,15,64,128]{3,2,1,0:T(8,128)S(1)} %get-tuple-element.16), channel_id=1, source_target_pairs={{0,4},{4,8},{8,12},{1,5},{5,9},{9,13},{2,6},{6,10},{10,14},{3,7},{... | collective-permute-start | bytes 4423688 | tf_op jit(solution)/shard_map/ppermute | solution.py:16
  53.9 1.3 collective-permute-start.5
  55.2 27.7 %collective-permute-done.4 = f32[3,15,64,128]{3,2,1,0:T(8,128)S(1)} collective-permute-done((f32[3,15,64,128]{3,2,1,0:T(8,128)S(1)}, f32[3,15,64,128]{3,2,1,0:T(8,128)S(1)}, u32[]{:S(2)}, u32[]{:S(2)}) %collective-permute-start.4) | collective-permute-done | bytes 1474592 | tf_op jit(solution)/shard_map/ppermute | solution.py:16
  82.9 4.2 %collective-permute-done.5 = f32[3,15,64,128]{3,2,1,0:T(8,128)S(1)} collective-permute-done((f32[3,15,64,128]{3,2,1,0:T(8,128)S(1)}, f32[3,15,64,128]{3,2,1,0:T(8,128)S(1)}, u32[]{:S(2)}, u32[]{:S(2)}) %collective-permute-start.5) | collective-permute-done | bytes 1474592 | tf_op jit(solution)/shard_map/ppermute | solution.py:17
  87.3 0.9 copy-done
  88.2 1.3 copy.12
  89.6 2.5 %collective-permute-start.6 = (f32[3,46,15,128]{3,1,2,0:T(8,128)}, f32[3,46,15,128]{3,1,2,0:T(8,128)}, u32[]{:S(2)}, u32[]{:S(2)}) collective-permute-start(f32[3,46,15,128]{3,1,2,0:T(8,128)} %copy.12), channel_id=1, source_target_pairs={{0,2},{1,3},{4,6},{5,7},{8,10},{9,11},{12,14},{13,15},{16,18},{17,... | collective-permute-start | bytes 3179528 | tf_op jit(solution)/shard_map/ppermute | solution.py:16
  92.0 1.3 copy.13
  93.3 1.5 collective-permute-start.7
  96.7 14.8 %collective-permute-done.6 = f32[3,46,15,128]{3,1,2,0:T(8,128)} collective-permute-done((f32[3,46,15,128]{3,1,2,0:T(8,128)}, f32[3,46,15,128]{3,1,2,0:T(8,128)}, u32[]{:S(2)}, u32[]{:S(2)}) %collective-permute-start.6) | collective-permute-done | bytes 1059872 | tf_op jit(solution)/shard_map/ppermute | solution.py:16
  111.5 1.6 %copy.14 = f32[3,46,15,128]{3,2,1,0:T(8,128)S(1)} copy(f32[3,46,15,128]{3,1,2,0:T(8,128)} %collective-permute-done.6) | data formatting | bytes 2119680 | tf_op jit(solution)/shard_map/ppermute | solution.py:16
  113.1 4.8 %collective-permute-done.7 = f32[3,46,15,128]{3,1,2,0:T(8,128)} collective-permute-done((f32[3,46,15,128]{3,1,2,0:T(8,128)}, f32[3,46,15,128]{3,1,2,0:T(8,128)}, u32[]{:S(2)}, u32[]{:S(2)}) %collective-permute-start.7) | collective-permute-done | bytes 1059872 | tf_op jit(solution)/shard_map/ppermute | solution.py:17
  117.9 1.6 %copy.15 = f32[3,46,15,128]{3,2,1,0:T(8,128)S(1)} copy(f32[3,46,15,128]{3,1,2,0:T(8,128)} %collective-permute-done.7) | data formatting | bytes 2119680 | tf_op jit(solution)/shard_map/ppermute | solution.py:17
  119.5 1.1 pad_maximum_fusion
  120.6 7.0 %fusion = f32[3,16,94,128]{3,1,2,0:T(8,128)S(1)} fusion(f32[3,46,94,128]{3,2,1,0:T(8,128)S(1)} %pad_maximum_fusion, f32[3,16,46,1]{2,0,1,3:T(4,128)S(1)} %convolution_bitcast_fusion.3), kind=kOutput, calls=%fused_computation | convolution fusion | flops 318799872 | bytes 8960640 | tf_op jit(solution)/shard_map/vij,vjyx->viyx/dot_general | solution.py:77
  127.7 2.4 %fusion.24 = f32[3,16,64,128]{3,2,1,0:T(8,128)S(1)} fusion(f32[3,16,94,128]{3,1,2,0:T(8,128)S(1)} %fusion, f32[3,64,94,1]{2,0,1,3:T(4,128)S(1)} %convolution_bitcast_fusion), kind=kOutput, calls=%fused_computation.26 | convolution fusion | flops 443547648 | bytes 3955200 | tf_op jit(solution)/shard_map/vij,vzjx->vzix/dot_general | solution.py:51
  130.1 3.7 %select_reduce_fusion = f32[16,64,128]{2,1,0:T(8,128)} fusion(f32[3,16,64,128]{3,2,1,0:T(8,128)S(1)} %fusion.24, pred[3]{0:T(512)(128)(4,1)S(1)} %compare_bitcast_fusion, f32[3,128,158,1]{1,0,2,3:T(4,128)S(1)} %fusion.35), kind=kOutput, calls=%fused_computation.24 | convolution fusion | flops 746192896 | bytes 2339843 | tf_op jit(solution)/shard_map/vzytj,vij->vzyti/dot_general | solution.py:46
  133.8 7.4 %all-gather.3.cloned.1.call-done = f32[32,64,128]{2,1,0:T(8,128)} async-done(((f32[16,64,128]{2,1,0:T(8,128)}), f32[32,64,128]{2,1,0:T(8,128)}) %all-gather.3.cloned.1.call-update) | async-done | bytes 1048592 | tf_op jit(solution)/shard_map/all_gather | solution.py:23
  141.3 2.1 %fusion.36 = f32[16,64,128]{2,1,0:T(8,128)} fusion(f32[16,64,128]{2,1,0:T(8,128)S(1)} %copy-done.2, f32[32,64,128]{2,1,0:T(8,128)} %all-gather.3.cloned.1.call-done), kind=kLoop, calls=%fused_computation.41 | loop fusion | flops 262144 | bytes 2097152 | tf_op jit(solution)/shard_map/mul | solution.py:82
  (32 shorter events, 3.4 us)
Async XLA Ops:
  6.5 7.7 %copy-start.3 = (f32[3,3,31]{2,1,0:T(4,128)S(1)}, f32[3,3,31]{2,1,0:T(4,128)}, u32[]{:S(2)}) copy-start(f32[3,3,31]{2,1,0:T(4,128)} %param.6) | copy-start | bytes 3352
  6.5 134.7 %all-gather.3.cloned.1.call-start = ((), (), s32[]{:S(2)}) async-start(), calls=%async_computation | async-start | bytes 1572864 | tf_op jit(solution)/shard_map/all_gather | solution.py:23
  8.0 16.1 %collective-permute-start = (f32[15,64,128]{2,0,1:T(8,128)S(1)}, f32[15,64,128]{2,0,1:T(8,128)S(1)}, u32[]{:S(2)}, u32[]{:S(2)}) collective-permute-start(f32[15,64,128]{2,0,1:T(8,128)S(1)} %get-tuple-element.20), channel_id=1, source_target_pairs={{0,4},{4,8},{8,12},{1,5},{5,9},{9,13},{2,6},{6,10},{10,14},{3,7},{... | collective-permute-start | bytes 1474568 | tf_op jit(solution)/shard_map/ppermute | solution.py:16
  12.9 15.3 %collective-permute-start.1 = (f32[15,64,128]{2,0,1:T(8,128)S(1)}, f32[15,64,128]{2,0,1:T(8,128)S(1)}, u32[]{:S(2)}, u32[]{:S(2)}) collective-permute-start(f32[15,64,128]{2,0,1:T(8,128)S(1)} %get-tuple-element.21), channel_id=1, source_target_pairs={{4,0},{8,4},{12,8},{5,1},{9,5},{13,9},{6,2},{10,6},{14,10},{7,3},{... | collective-permute-start | bytes 1474568 | tf_op jit(solution)/shard_map/ppermute | solution.py:17
  28.3 10.0 %collective-permute-start.2 = (f32[46,15,128]{2,0,1:T(8,128)S(1)}, f32[46,15,128]{2,0,1:T(8,128)S(1)}, u32[]{:S(2)}, u32[]{:S(2)}) collective-permute-start(f32[46,15,128]{2,0,1:T(8,128)S(1)} %get-tuple-element.18), channel_id=1, source_target_pairs={{0,2},{1,3},{4,6},{5,7},{8,10},{9,11},{12,14},{13,15},{16,18},{17,... | collective-permute-start | bytes 1059848 | tf_op jit(solution)/shard_map/ppermute | solution.py:16
  31.7 10.8 %collective-permute-start.3 = (f32[46,15,128]{2,0,1:T(8,128)S(1)}, f32[46,15,128]{2,0,1:T(8,128)S(1)}, u32[]{:S(2)}, u32[]{:S(2)}) collective-permute-start(f32[46,15,128]{2,0,1:T(8,128)S(1)} %get-tuple-element.19), channel_id=1, source_target_pairs={{2,0},{3,1},{6,4},{7,5},{10,8},{11,9},{14,12},{15,13},{18,16},{19,... | collective-permute-start | bytes 1059848 | tf_op jit(solution)/shard_map/ppermute | solution.py:17
  44.5 2.4 %copy-start.4 = (f32[3,16,64,128]{3,2,1,0:T(8,128)S(1)}, f32[3,16,64,128]{3,2,1,0:T(8,128)}, u32[]{:S(2)}) copy-start(f32[3,16,64,128]{3,2,1,0:T(8,128)} %param.4) | copy-start | bytes 4718596
  50.3 32.6 %collective-permute-start.4 = (f32[3,15,64,128]{3,2,1,0:T(8,128)S(1)}, f32[3,15,64,128]{3,2,1,0:T(8,128)S(1)}, u32[]{:S(2)}, u32[]{:S(2)}) collective-permute-start(f32[3,15,64,128]{3,2,1,0:T(8,128)S(1)} %get-tuple-element.16), channel_id=1, source_target_pairs={{0,4},{4,8},{8,12},{1,5},{5,9},{9,13},{2,6},{6,10},{10,14},{3,7},{... | collective-permute-start | bytes 4423688 | tf_op jit(solution)/shard_map/ppermute | solution.py:16
  53.9 33.2 %collective-permute-start.5 = (f32[3,15,64,128]{3,2,1,0:T(8,128)S(1)}, f32[3,15,64,128]{3,2,1,0:T(8,128)S(1)}, u32[]{:S(2)}, u32[]{:S(2)}) collective-permute-start(f32[3,15,64,128]{3,2,1,0:T(8,128)S(1)} %get-tuple-element.17), channel_id=1, source_target_pairs={{4,0},{8,4},{12,8},{5,1},{9,5},{13,9},{6,2},{10,6},{14,10},{7,3},{... | collective-permute-start | bytes 4423688 | tf_op jit(solution)/shard_map/ppermute | solution.py:17
  87.1 1.1 copy-start
  89.6 21.9 %collective-permute-start.6 = (f32[3,46,15,128]{3,1,2,0:T(8,128)}, f32[3,46,15,128]{3,1,2,0:T(8,128)}, u32[]{:S(2)}, u32[]{:S(2)}) collective-permute-start(f32[3,46,15,128]{3,1,2,0:T(8,128)} %copy.12), channel_id=1, source_target_pairs={{0,2},{1,3},{4,6},{5,7},{8,10},{9,11},{12,14},{13,15},{16,18},{17,... | collective-permute-start | bytes 3179528 | tf_op jit(solution)/shard_map/ppermute | solution.py:16
  92.0 4.6 %copy-start.5 = (s32[3,1,1]{0,2,1:T(1,128)S(1)}, s32[3,1,1]{0,2,1:T(1,128)}, u32[]{:S(2)}) copy-start(s32[3,1,1]{0,2,1:T(1,128)} %param.7) | copy-start | bytes 40
  93.3 24.6 %collective-permute-start.7 = (f32[3,46,15,128]{3,1,2,0:T(8,128)}, f32[3,46,15,128]{3,1,2,0:T(8,128)}, u32[]{:S(2)}, u32[]{:S(2)}) collective-permute-start(f32[3,46,15,128]{3,1,2,0:T(8,128)} %copy.13), channel_id=1, source_target_pairs={{2,0},{3,1},{6,4},{7,5},{10,8},{11,9},{14,12},{15,13},{18,16},{19,... | collective-permute-start | bytes 3179528 | tf_op jit(solution)/shard_map/ppermute | solution.py:17
  113.1 6.4 %copy-start.1 = (f32[3,15,64,128]{3,2,1,0:T(8,128)S(1)}, f32[3,15,64,128]{3,2,1,0:T(8,128)}, u32[]{:S(2)}) copy-start(f32[3,15,64,128]{3,2,1,0:T(8,128)} %copy-done) | copy-start | bytes 4423684
  130.1 11.2 %copy-start.2 = (f32[16,64,128]{2,1,0:T(8,128)S(1)}, f32[16,64,128]{2,1,0:T(8,128)}, u32[]{:S(2)}) copy-start(f32[16,64,128]{2,1,0:T(8,128)} %param.5) | copy-start | bytes 1572868
Sparse Core Ops, SparseCore 0:
  134.0 7.2 all-gather.2
where the time goes:
time: 151 us; the launch traced here: 150 us
  waiting for transfers between devices  80.7 us (53%)
  matrix products  23.6 us (16%)
  starting transfers between devices  19.7 us (13%)
  between operations  13.7 us (9%)
  local copies, waits for them, and re-layouts  8.89 us (6%)
  other arithmetic  3.64 us (2%)
    ppermute x4, waiting for transfers between devices, padded_2(): before = lax.ppermute(last, axis, up)  55.9 us
    ppermute x4, waiting for transfers between devices, padded_2(): after = lax.ppermute(first, axis, down)  17.3 us
    ppermute x4, starting transfers between devices, padded_2(): before = lax.ppermute(last, axis, up)  14.4 us
    all_gather x1, waiting for transfers between devices, joined(): pieces = lax.all_gather(value, axis)  7.42 us
    dot_general x1, matrix products, body(): jnp.einsum('vij,vjyx->viyx', back_z, ratio_pad, precision=lax.Precision.H...  7.03 us
    dot_general x2, matrix products, x_pass(): jnp.einsum('vzytj,vij->vzyti', stacked, x_band, precision=lax.Precision.H...  6.69 us
    ppermute x4, starting transfers between devices, padded_2(): after = lax.ppermute(first, axis, down)  5.34 us
    dot_general x2, matrix products, finish_blur(): jnp.einsum('vij,vzjx->vzix', y_band, along_z, precision=lax.Precision.HIG...  4.8 us
  transfers between devices with their start and end apart: 9, of which 9 were waited for; matrix products, arithmetic and copies ran while one was open for 4% of the time, Pallas kernels for 0%

commit v1 on v0

v1 whole, which is shorter than its diff:
```python
import functools

import jax
import jax.numpy as jnp
from jax import lax
from jax.experimental import pallas as pl
from jax.experimental.pallas import tpu as pltpu
from jax.sharding import PartitionSpec as P

HALF = 15
TAPS = 2 * HALF + 1
PAD = HALF + 1
PARTS = 4


def split(value):
    high = value.astype(jnp.bfloat16)
    low = (value - high.astype(jnp.float32)).astype(jnp.bfloat16)
    return high, low


def kernel(sizes, zpeers, ypeers, psf, cov, images_hbm, est_hbm, out,
           fpad, gz_out, images, rpad, cpad, acc, other,
           wzf, wzb, wyf, wyb, wxf, wxb, send, recv, local_sem):
    views, depth, height, width = sizes
    zext, yext = depth + 2 * PAD, height + 2 * PAD
    zi, yi, ci = lax.axis_index("gz"), lax.axis_index("gy"), lax.axis_index("view")
    has = {("gz", 1): zi < zpeers - 1, ("gz", -1): zi > 0,
           ("gy", 1): yi < ypeers - 1, ("gy", -1): yi > 0}
    index = {"gz": zi, "gy": yi}
    sides = ((1, 0), (-1, 1))
    far = {"gz": depth, "gy": height}

    def target(axis, side):
        return {axis: index[axis] + side}

    images_copy = pltpu.make_async_copy(images_hbm, images, local_sem.at[0])
    est_copy = pltpu.make_async_copy(
        est_hbm, fpad.at[pl.ds(PAD, depth), pl.ds(PAD, height), :], local_sem.at[1])
    images_copy.start()
    est_copy.start()

    barrier = pltpu.get_barrier_semaphore()
    for (axis, side), there in has.items():
        @pl.when(there)
        def _(axis=axis, side=side):
            pl.semaphore_signal(barrier, inc=1, device_id=target(axis, side),
                                device_id_type=pl.DeviceIdType.MESH)
    pl.semaphore_signal(barrier, inc=1, device_id={"view": 1 - ci},
                        device_id_type=pl.DeviceIdType.MESH)
    count = 1
    for there in has.values():
        count = count + there.astype(jnp.int32)
    pl.semaphore_wait(barrier, count)

    slots = iter(range(64))

    class Remote:
        def __init__(self, axis, side, src, dst):
            slot = next(slots)
            self.axis, self.side = axis, side
            self.copy = pltpu.make_async_remote_copy(
                src_ref=src, dst_ref=dst, send_sem=send.at[slot], recv_sem=recv.at[slot],
                device_id=target(axis, side), device_id_type=pl.DeviceIdType.MESH)

        def start(self):
            pl.when(has[self.axis, self.side])(self.copy.start)

        def wait_recv(self):
            pl.when(has[self.axis, -self.side])(self.copy.wait_recv)

        def wait_send(self):
            pl.when(has[self.axis, self.side])(self.copy.wait_send)

    zsrc = {1: depth - HALF, -1: 0}
    zdst = {1: 1, -1: PAD + depth}
    ysrc = {1: height - PAD, -1: 0}
    ydst = {1: 0, -1: PAD + height}

    f_z = [Remote("gz", s, est_hbm.at[pl.ds(zsrc[s], HALF)],
                  fpad.at[pl.ds(zdst[s], HALF), pl.ds(PAD, height), :]) for s, _ in sides]
    f_y = [Remote("gy", s, est_hbm.at[:, pl.ds(ysrc[s], PAD), :],
                  fpad.at[pl.ds(PAD, depth), pl.ds(ydst[s], PAD), :]) for s, _ in sides]
    f_c = {zs: [Remote("gy", s, fpad.at[pl.ds(zdst[zs], HALF), pl.ds(PAD + ysrc[s], PAD), :],
                       fpad.at[pl.ds(zdst[zs], HALF), pl.ds(ydst[s], PAD), :]) for s, _ in sides]
           for zs, _ in sides}

    def ratio_halo(v, s, first, rows):
        return Remote("gz", s,
                      rpad.at[v, pl.ds(PAD + zsrc[s], HALF), pl.ds(first, rows), :],
                      rpad.at[v, pl.ds(zdst[s], HALF), pl.ds(first, rows), :])

    r_outer = [[ratio_halo(v, s, first, PAD) for s, _ in sides for first in (0, height - PAD)]
               for v in range(views)]
    r_mid = [[ratio_halo(v, s, PAD, height - 2 * PAD) for s, _ in sides] for v in range(views)]
    c_y = [[Remote("gy", s, cpad.at[v, :, pl.ds(PAD + ysrc[s], PAD), :],
                   cpad.at[v, :, pl.ds(ydst[s], PAD), :]) for s, _ in sides]
           for v in range(views)]

    for c in f_z + f_y:
        c.start()

    for k in (0, zext - 1):
        fpad[k] = jnp.zeros((yext, width), jnp.float32)
        for v in range(views):
            rpad[v, k] = jnp.zeros((height, width), jnp.float32)
    for s, _ in sides:
        @pl.when(jnp.logical_not(has["gz", -s]))
        def _(s=s):
            @pl.loop(0, HALF)
            def _(k):
                fpad[zdst[s] + k] = jnp.zeros((yext, width), jnp.float32)
                for v in range(views):
                    rpad[v, zdst[s] + k] = jnp.zeros((height, width), jnp.float32)

        @pl.when(jnp.logical_not(has["gy", -s]))
        def _(s=s):
            @pl.loop(0, zext)
            def _(k):
                fpad[k, pl.ds(ydst[s], PAD), :] = jnp.zeros((PAD, width), jnp.float32)

            @pl.loop(0, depth)
            def _(k):
                for v in range(views):
                    cpad[v, k, pl.ds(ydst[s], PAD), :] = jnp.zeros((PAD, width), jnp.float32)

    def bands(v, axis, shape, offset):
        def step(t, carry):
            fwd, back = carry
            tap = psf[v, axis, t]
            return (jnp.where(offset == t, tap, fwd), jnp.where(offset == TAPS - 1 - t, tap, back))
        zero = jnp.zeros(shape, jnp.float32)
        fwd, back = lax.fori_loop(0, TAPS, step, (zero, zero))
        total = lax.fori_loop(0, TAPS, lambda t, s: s + psf[v, axis, t], jnp.float32(0.0))
        total = jnp.full(shape, total, jnp.float32)
        return split(fwd / total), split(back / total)

    def banded(rows, ext):
        shape = (rows, 2 * ext)
        row = lax.broadcasted_iota(jnp.int32, shape, 0)
        col = lax.broadcasted_iota(jnp.int32, shape, 1)
        col = jnp.where(col >= ext, col - ext, col)
        return shape, col - row - (PAD - HALF)

    for v in range(views):
        (fh, fl), (bh, bl) = bands(v, 0, *banded(depth, zext))
        wzf[pl.ds(v * depth, depth), :] = fh
        wzf[pl.ds((views + v) * depth, depth), :] = fl
        wzb[v, pl.ds(0, depth), :] = bh
        wzb[v, pl.ds(depth, depth), :] = bl
        (fh, fl), (bh, bl) = bands(v, 1, *banded(height, yext))
        wyf[v, pl.ds(0, height), :] = fh
        wyf[v, pl.ds(height, height), :] = fl
        wyb[v, pl.ds(0, height), :] = bh
        wyb[v, pl.ds(height, height), :] = bl
        shape = (width, width)
        offset = (lax.broadcasted_iota(jnp.int32, shape, 0)
                  - lax.broadcasted_iota(jnp.int32, shape, 1) + HALF)
        (fh, fl), (bh, bl) = bands(v, 2, shape, offset)
        for k in range(2):
            wxf[v, pl.ds(k * width, width), pl.ds(0, width)] = fh
            wxf[v, pl.ds(k * width, width), pl.ds(width, width)] = fl
            wxb[v, pl.ds(k * width, width), pl.ds(0, width)] = bh
            wxb[v, pl.ds(k * width, width), pl.ds(width, width)] = bl

    def left(weights, pieces):
        high, low = split(jnp.concatenate(pieces, axis=1))
        both = jnp.dot(weights, jnp.concatenate([high, low], axis=0),
                       preferred_element_type=jnp.float32)
        half = both.shape[0] // 2
        return both[:half] + both[half:]

    def right(value, weights):
        high, low = split(value)
        both = jnp.dot(jnp.concatenate([high, low], axis=1), weights,
                       preferred_element_type=jnp.float32)
        return both[:, :width] + both[:, width:]

    def z_pass(weights, src, src_first, src_stride, dst, dst_first, dst_stride, planes, first, rows):
        group = 4

        def step(k, carry):
            y = first + k * group
            pieces = [src[pl.ds(src_first + y + j, zext, stride=src_stride), :] for j in range(group)]
            result = left(weights, pieces)
            for j in range(group):
                dst[pl.ds(dst_first + y + j, planes, stride=dst_stride), :] = (
                    result[:, j * width:(j + 1) * width])
            return carry
        lax.fori_loop(0, rows // group, step, 0)

    f2 = fpad.reshape(zext * yext, width)
    g2 = gz_out.reshape(views * depth * yext, width)
    r2 = rpad.reshape(views * zext * height, width)
    c2 = cpad.reshape(views * depth * yext, width)

    def forward_z(first, rows):
        z_pass(wzf[...], f2, 0, yext, g2, 0, yext, views * depth, first, rows)

    def backward_z(v, first, rows):
        z_pass(wzb[v], r2, v * zext * height, height, c2, v * depth * yext + PAD, yext, depth,
               first, rows)

    est_copy.wait()
    for (s, _), c in zip(sides, f_z):
        c.wait_recv()
    for zs, _ in sides:
        @pl.when(has["gz", -zs])
        def _(zs=zs):
            for c in f_c[zs]:
                c.start()
    forward_z(PAD, height)
    for c in f_y:
        c.wait_recv()
    for zs, _ in sides:
        @pl.when(has["gz", -zs])
        def _(zs=zs):
            for c in f_c[zs]:
                c.wait_recv()
    forward_z(0, PAD)
    forward_z(PAD + height, PAD)
    images_copy.wait()

    def ratio(v):
        def step(k, carry):
            z = 2 * k
            along_y = left(wyf[v], [gz_out[v * depth + z + j] for j in range(2)])
            rows = jnp.concatenate([along_y[:, :width], along_y[:, width:]], axis=0)
            blurred = right(rows, wxf[v])
            image = jnp.concatenate([images[v, z], images[v, z + 1]], axis=0)
            result = right(image / blurred, wxb[v])
            rpad[v, PAD + z] = result[:height]
            rpad[v, PAD + z + 1] = result[height:]
            return carry
        lax.fori_loop(0, depth // 2, step, 0)

    def start(group):
        for c in group:
            c.start()

    for v in range(views):
        ratio(v)
        start(r_outer[v])
        if v == 0:
            start(r_mid[v])
    for v in range(1, views):
        start(r_mid[v])

    def correction(v, first, planes):
        covered = jnp.full((height, width), cov[v, 0, 0], jnp.int32) > 0

        def step(k, carry):
            z = first + 2 * k
            result = left(wyb[v], [cpad[v, z + j] for j in range(2)])
            for j in range(2):
                masked = jnp.where(covered, result[:, j * width:(j + 1) * width], jnp.float32(1.0))
                acc[z + j] = masked if v == 0 else acc[z + j] * masked
            return carry
        lax.fori_loop(0, planes // 2, step, 0)

    def outer(v):
        for c in r_outer[v]:
            c.wait_recv()
        backward_z(v, 0, PAD)
        backward_z(v, height - PAD, PAD)
        start(c_y[v])

    def mid(v):
        for c in r_mid[v]:
            c.wait_recv()
        backward_z(v, PAD, height - 2 * PAD)
        for c in c_y[v]:
            c.wait_recv()

    outer(0)
    mid(0)
    correction(0, 0, depth)
    for v in range(1, views):
        outer(v)
    for v in range(1, views - 1):
        mid(v)
        correction(v, 0, depth)
    mid(views - 1)

    per = depth // PARTS
    exchange = []
    for k in range(PARTS):
        correction(views - 1, k * per, per)
        slot = next(slots)
        part = pltpu.make_async_remote_copy(
            src_ref=acc.at[pl.ds(k * per, per)], dst_ref=other.at[pl.ds(k * per, per)],
            send_sem=send.at[slot], recv_sem=recv.at[slot],
            device_id={"view": 1 - ci}, device_id_type=pl.DeviceIdType.MESH)
        part.start()
        exchange.append(part)
    for k, part in enumerate(exchange):
        part.wait_recv()

        def step(z, carry):
            out[z] = fpad[PAD + z, pl.ds(PAD, height), :] * (acc[z] * other[z])
            return carry
        lax.fori_loop(k * per, (k + 1) * per, step, 0)

    for c in f_z + f_y:
        c.wait_send()
    for zs, _ in sides:
        @pl.when(has["gz", -zs])
        def _(zs=zs):
            for c in f_c[zs]:
                c.wait_send()
    for v in range(views):
        for c in r_outer[v] + r_mid[v] + c_y[v]:
            c.wait_send()
    for part in exchange:
        part.wait_send()


def solution(mesh):
    zpeers, ypeers = mesh.shape["gz"], mesh.shape["gy"]

    def body(images, estimate, psf, coverage):
        views, depth, height, width = images.shape
        zext, yext = depth + 2 * PAD, height + 2 * PAD
        f32, bf16 = jnp.float32, jnp.bfloat16
        return pl.pallas_call(
            functools.partial(kernel, images.shape, zpeers, ypeers),
            out_shape=jax.ShapeDtypeStruct(estimate.shape, f32),
            in_specs=[
                pl.BlockSpec(memory_space=pltpu.SMEM),
                pl.BlockSpec(memory_space=pltpu.SMEM),
                pl.BlockSpec(memory_space=pl.ANY),
                pl.BlockSpec(memory_space=pl.ANY),
            ],
            out_specs=pl.BlockSpec(memory_space=pltpu.VMEM),
            scratch_shapes=[
                pltpu.VMEM((zext, yext, width), f32),
                pltpu.VMEM((views * depth, yext, width), f32),
                pltpu.VMEM(images.shape, f32),
                pltpu.VMEM((views, zext, height, width), f32),
                pltpu.VMEM((views, depth, yext, width), f32),
                pltpu.VMEM(estimate.shape, f32),
                pltpu.VMEM(estimate.shape, f32),
                pltpu.VMEM((2 * views * depth, 2 * zext), bf16),
                pltpu.VMEM((views, 2 * depth, 2 * zext), bf16),
                pltpu.VMEM((views, 2 * height, 2 * yext), bf16),
                pltpu.VMEM((views, 2 * height, 2 * yext), bf16),
                pltpu.VMEM((views, 2 * width, 2 * width), bf16),
                pltpu.VMEM((views, 2 * width, 2 * width), bf16),
                pltpu.SemaphoreType.DMA((64,)),
                pltpu.SemaphoreType.DMA((64,)),
                pltpu.SemaphoreType.DMA((2,)),
            ],
            compiler_params=pltpu.CompilerParams(
                collective_id=0, has_side_effects=True, vmem_limit_bytes=40 * 2**20),
        )(psf, coverage, images, estimate)

    return jax.shard_map(
        body,
        mesh=mesh,
        in_specs=(
            P("view", ("tile", "gz"), "gy", None),
            P(("tile", "gz"), "gy", None),
            P("view", None, None),
            P("view", ("tile", "gz"), "gy"),
        ),
        out_specs=P(("tile", "gz"), "gy", None),
        check_vma=False,
    )
```

time: 151 us -> 70.9 us (0.47)
  waiting for transfers between devices: 80.7 us -> 0 us
  Pallas kernels: 0 us -> 66 us
  matrix products: 23.6 us -> 0 us
  starting transfers between devices: 19.7 us -> 0 us
  between operations: 13.7 us -> 0.01 us
  local copies, waits for them, and re-layouts: 8.89 us -> 4.68 us
  other arithmetic: 3.64 us -> 0 us
    ppermute x8 -> x0, waiting for transfers between devices: 73.2 us -> none  [the longest x4 55.9 us: padded_2(): before = lax.ppermute(last, axis, up)]
    pallas_call x0 -> x1, Pallas kernels: none -> 66 us  [body(): pl.pallas_call(functools.partial(kernel, images.shape, zpeers, ypeers), o...]
    dot_general x12 -> x0, matrix products: 23.6 us -> none  [the longest x1 7.03 us: body(): jnp.einsum('vij,vjyx->viyx', back_z, ratio_pad, precision=lax.Precision.H...]
    ppermute x8 -> x0, starting transfers between devices: 19.7 us -> none  [the longest x4 14.4 us: padded_2(): before = lax.ppermute(last, axis, up)]
    all_gather x1 -> x0, waiting for transfers between devices: 7.42 us -> none  [joined(): pieces = lax.all_gather(value, axis)]
    slice x8 -> x0, local copies, waits for them, and re-layouts: 3.36 us -> none  [the longest x3 1.75 us: padded_2(): last = lax.slice_in_dim(x, length - width, length, axis=dim)]
    ppermute x2 -> x0, local copies, waits for them, and re-layouts: 3.21 us -> none  [the longest x1 1.61 us: padded_2(): after = lax.ppermute(first, axis, down)]
    unnamed x13 -> x8, local copies, waits for them, and re-layouts: 2.32 us -> 4.68 us
  transfers between devices with their start and end apart: 9 -> 0, of which waited for: 9 -> 0; matrix products, arithmetic and copies ran while one was open for 4% -> 0% of each run, Pallas kernels for 0% -> 0%
where the time goes in v1:
time: 70.9 us; the launch traced here: 70.7 us
  Pallas kernels  66 us (93%)
  local copies, waits for them, and re-layouts  4.68 us (7%)
    pallas_call x1, Pallas kernels, body(): pl.pallas_call(functools.partial(kernel, images.shape, zpeers, ypeers), o...  66 us
    unnamed x8, local copies, waits for them, and re-layouts  4.68 us

profile of v1, /device:TPU:0, one launch (start us, length us, event | category | flops | bytes accessed | tf_op | source)
XLA Modules:
  0.0 70.7 jit_solution(8716074726164807337)
XLA Ops:
  0.0 0.7 %copy.5.cov = s32[3,1,1]{2,1,0:T(1,128)S(1)} copy(s32[3,1,1]{0,2,1:T(1,128)} %param.7) | data formatting | bytes 24 | tf_op args[3]
  0.7 0.0 copy-start
  0.7 1.4 %copy-done = f32[3,16,64,128]{3,2,1,0:T(8,128)S(1)} copy-done((f32[3,16,64,128]{3,2,1,0:T(8,128)S(1)}, f32[3,16,64,128]{3,2,1,0:T(8,128)}, u32[]{:S(2)}) %copy-start) | copy-done | bytes 1572888
  2.1 0.0 copy-start.1
  2.2 1.0 %copy-done.1 = f32[16,64,128]{2,1,0:T(8,128)S(1)} copy-done((f32[16,64,128]{2,1,0:T(8,128)S(1)}, f32[16,64,128]{2,1,0:T(8,128)}, u32[]{:S(2)}) %copy-start.1) | copy-done | bytes 524312
  3.2 0.0 copy-start.2
  3.2 0.7 copy-done.2
  3.9 66.0 %shard_map.46 = f32[16,64,128]{2,1,0:T(8,128)S(1)} custom-call(f32[3,3,31]{2,1,0:T(4,128)S(1)} %copy-done.2, s32[3,1,1]{2,1,0:T(1,128)S(1)} %copy.5.cov, f32[3,16,64,128]{3,2,1,0:T(8,128)S(1)} %copy-done, f32[16,64,128]{2,1,0:T(8,128)S(1)} %copy-done.1), custom_call_target="tpu_custom_call" | custom-call | tf_op jit(solution)/shard_map/pallas_call | solution.py:325
  69.9 0.8 %copy.7 = f32[16,64,128]{2,1,0:T(8,128)} copy(f32[16,64,128]{2,1,0:T(8,128)S(1)} %shard_map.46) | data formatting | bytes 1048576
Async XLA Ops:
  0.7 1.4 %copy-start = (f32[3,16,64,128]{3,2,1,0:T(8,128)S(1)}, f32[3,16,64,128]{3,2,1,0:T(8,128)}, u32[]{:S(2)}) copy-start(f32[3,16,64,128]{3,2,1,0:T(8,128)} %images_hbm.1) | copy-start | bytes 4718596
  2.1 1.0 %copy-start.1 = (f32[16,64,128]{2,1,0:T(8,128)S(1)}, f32[16,64,128]{2,1,0:T(8,128)}, u32[]{:S(2)}) copy-start(f32[16,64,128]{2,1,0:T(8,128)} %est_hbm.1) | copy-start | bytes 1572868
  3.2 0.7 copy-start.2

commit v2 on v1

--- a/solution.py
+++ b/solution.py
@@ -21,7 +21,7 @@
 
 def kernel(sizes, zpeers, ypeers, psf, cov, images_hbm, est_hbm, out,
            fpad, gz_out, images, rpad, cpad, acc, other,
-           wzf, wzb, wyf, wyb, wxf, wxb, send, recv, local_sem):
+           wzf, wzb, wyf, wyb, wym, wyo, wxf, wxb, send, recv, local_sem):
     views, depth, height, width = sizes
     zext, yext = depth + 2 * PAD, height + 2 * PAD
     zi, yi, ci = lax.axis_index("gz"), lax.axis_index("gy"), lax.axis_index("view")
@@ -72,13 +72,35 @@
         def wait_send(self):
             pl.when(has[self.axis, self.side])(self.copy.wait_send)
 
+    class Share:
+        def __init__(self, side, ref):
+            slot = next(slots)
+            self.side = side
+            self.copy = pltpu.make_async_remote_copy(
+                src_ref=ref, dst_ref=ref, send_sem=send.at[slot], recv_sem=recv.at[slot],
+                device_id={"view": 1 - ci}, device_id_type=pl.DeviceIdType.MESH)
+
+        def start(self):
+            pl.when(has["gz", -self.side])(self.copy.start)
+
+        def wait_recv(self):
+            pl.when(has["gz", -self.side])(self.copy.wait_recv)
+
+        def wait_send(self):
+            pl.when(has["gz", -self.side])(self.copy.wait_send)
+
     zsrc = {1: depth - HALF, -1: 0}
     zdst = {1: 1, -1: PAD + depth}
     ysrc = {1: height - PAD, -1: 0}
     ydst = {1: 0, -1: PAD + height}
 
-    f_z = [Remote("gz", s, est_hbm.at[pl.ds(zsrc[s], HALF)],
-                  fpad.at[pl.ds(zdst[s], HALF), pl.ds(PAD, height), :]) for s, _ in sides]
+    quarter = height // 4
+    fetched = (pl.multiple_of(ci * (height - quarter), 8), pl.multiple_of(quarter + ci * quarter, 8))
+    f_z = [[Remote("gz", s, est_hbm.at[pl.ds(zsrc[s], HALF), pl.ds(row, quarter), :],
+                   fpad.at[pl.ds(zdst[s], HALF), pl.ds(PAD + row, quarter), :]) for s, _ in sides]
+           for row in fetched]
+    f_s = [[Share(s, fpad.at[pl.ds(zdst[s], HALF), pl.ds(PAD + row, quarter), :]) for s, _ in sides]
+           for row in fetched]
     f_y = [Remote("gy", s, est_hbm.at[:, pl.ds(ysrc[s], PAD), :],
                   fpad.at[pl.ds(PAD, depth), pl.ds(ydst[s], PAD), :]) for s, _ in sides]
     f_c = {zs: [Remote("gy", s, fpad.at[pl.ds(zdst[zs], HALF), pl.ds(PAD + ysrc[s], PAD), :],
@@ -92,12 +114,15 @@
 
     r_outer = [[ratio_halo(v, s, first, PAD) for s, _ in sides for first in (0, height - PAD)]
                for v in range(views)]
-    r_mid = [[ratio_halo(v, s, PAD, height - 2 * PAD) for s, _ in sides] for v in range(views)]
+    inner = height - 2 * PAD
+    r_mid = [[ratio_halo(v, s, PAD, inner) for s, _ in sides] for v in range(views - 1)]
+    r_last = [[ratio_halo(views - 1, s, PAD + k * inner // 2, inner // 2) for s, _ in sides]
+              for k in range(2)]
     c_y = [[Remote("gy", s, cpad.at[v, :, pl.ds(PAD + ysrc[s], PAD), :],
                    cpad.at[v, :, pl.ds(ydst[s], PAD), :]) for s, _ in sides]
            for v in range(views)]
 
-    for c in f_z + f_y:
+    for c in f_z[0] + f_y + f_z[1]:
         c.start()
 
     for k in (0, zext - 1):
@@ -126,12 +151,12 @@
 
     def bands(v, axis, shape, offset):
         def step(t, carry):
-            fwd, back = carry
+            fwd, back, total = carry
             tap = psf[v, axis, t]
-            return (jnp.where(offset == t, tap, fwd), jnp.where(offset == TAPS - 1 - t, tap, back))
+            return (jnp.where(offset == t, tap, fwd),
+                    jnp.where(offset == TAPS - 1 - t, tap, back), total + tap)
         zero = jnp.zeros(shape, jnp.float32)
-        fwd, back = lax.fori_loop(0, TAPS, step, (zero, zero))
-        total = lax.fori_loop(0, TAPS, lambda t, s: s + psf[v, axis, t], jnp.float32(0.0))
+        fwd, back, total = lax.fori_loop(0, TAPS, step, (zero, zero, jnp.float32(0.0)), unroll=True)
         total = jnp.full(shape, total, jnp.float32)
         return split(fwd / total), split(back / total)
 
@@ -142,17 +167,22 @@
         col = jnp.where(col >= ext, col - ext, col)
         return shape, col - row - (PAD - HALF)
 
-    for v in range(views):
+    def z_bands(v):
         (fh, fl), (bh, bl) = bands(v, 0, *banded(depth, zext))
         wzf[pl.ds(v * depth, depth), :] = fh
         wzf[pl.ds((views + v) * depth, depth), :] = fl
         wzb[v, pl.ds(0, depth), :] = bh
         wzb[v, pl.ds(depth, depth), :] = bl
+
+    def y_bands(v):
         (fh, fl), (bh, bl) = bands(v, 1, *banded(height, yext))
-        wyf[v, pl.ds(0, height), :] = fh
-        wyf[v, pl.ds(height, height), :] = fl
         wyb[v, pl.ds(0, height), :] = bh
         wyb[v, pl.ds(height, height), :] = bl
+        if v > 0:
+            wyf[v, pl.ds(0, height), :] = fh
+            wyf[v, pl.ds(height, height), :] = fl
+
+    def x_bands(v):
         shape = (width, width)
         offset = (lax.broadcasted_iota(jnp.int32, shape, 0)
                   - lax.broadcasted_iota(jnp.int32, shape, 1) + HALF)
@@ -163,6 +193,14 @@
             wxb[v, pl.ds(k * width, width), pl.ds(0, width)] = bh
             wxb[v, pl.ds(k * width, width), pl.ds(width, width)] = bl
 
+    def part_bands():
+        (fh, fl), _ = bands(0, 1, *banded(inner, height))
+        wym[pl.ds(0, inner), :] = fh
+        wym[pl.ds(inner, inner), :] = fl
+        (fh, fl), _ = bands(0, 1, *banded(PAD, 3 * PAD))
+        wyo[pl.ds(0, PAD), :] = fh
+        wyo[pl.ds(PAD, PAD), :] = fl
+
     def left(weights, pieces):
         high, low = split(jnp.concatenate(pieces, axis=1))
         both = jnp.dot(weights, jnp.concatenate([high, low], axis=0),
@@ -177,7 +215,7 @@
         return both[:, :width] + both[:, width:]
 
     def z_pass(weights, src, src_first, src_stride, dst, dst_first, dst_stride, planes, first, rows):
-        group = 4
+        group = 8
 
         def step(k, carry):
             y = first + k * group
@@ -201,15 +239,63 @@
         z_pass(wzb[v], r2, v * zext * height, height, c2, v * depth * yext + PAD, yext, depth,
                first, rows)
 
+    for v in range(views):
+        z_bands(v)
     est_copy.wait()
-    for (s, _), c in zip(sides, f_z):
-        c.wait_recv()
-    for zs, _ in sides:
-        @pl.when(has["gz", -zs])
-        def _(zs=zs):
-            for c in f_c[zs]:
-                c.start()
+    for k in range(2):
+        for c, d in zip(f_z[k], f_s[k]):
+            c.wait_recv()
+            d.start()
+        if k == 0:
+            part_bands()
+            for d in f_s[0]:
+                d.wait_recv()
+            for zs, _ in sides:
+                @pl.when(has["gz", -zs])
+                def _(zs=zs):
+                    for c in f_c[zs]:
+                        c.start()
+            x_bands(0)
+    for d in f_s[1]:
+        d.wait_recv()
     forward_z(PAD, height)
+    images_copy.wait()
+
+    def ratio(v, weights, blocks, first, rows):
+        planes = 4
+
+        def step(k, carry):
+            z = planes * k
+            along_y = left(weights, [gz_out[v * depth + z + j, pl.ds(b, n), :]
+                                     for j in range(planes) for b, n in blocks])
+            count = planes * len(blocks)
+            lines = jnp.concatenate([along_y[:, j * width:(j + 1) * width] for j in range(count)],
+                                    axis=0)
+            blurred = right(lines, wxf[v])
+            image = jnp.concatenate([images[v, z + j, pl.ds(f, rows), :]
+                                     for j in range(planes) for f in first], axis=0)
+            result = right(image / blurred, wxb[v])
+            at = 0
+            for j in range(planes):
+                for f in first:
+                    rpad[v, PAD + z + j, pl.ds(f, rows), :] = result[at:at + rows]
+                    at += rows
+            return carry
+        lax.fori_loop(0, depth // planes, step, 0)
+
+    def start(group):
+        for c in group:
+            c.start()
+
+    def sent(group):
+        for c in group:
+            c.wait_send()
+
+    def whole(v):
+        ratio(v, wyf[v], [(0, yext)], [0], height)
+
+    ratio(0, wym[...], [(PAD, height)], [PAD], inner)
+    start(r_mid[0])
     for c in f_y:
         c.wait_recv()
     for zs, _ in sides:
@@ -219,44 +305,27 @@
                 c.wait_recv()
     forward_z(0, PAD)
     forward_z(PAD + height, PAD)
-    images_copy.wait()
-
-    def ratio(v):
-        def step(k, carry):
-            z = 2 * k
-            along_y = left(wyf[v], [gz_out[v * depth + z + j] for j in range(2)])
-            rows = jnp.concatenate([along_y[:, :width], along_y[:, width:]], axis=0)
-            blurred = right(rows, wxf[v])
-            image = jnp.concatenate([images[v, z], images[v, z + 1]], axis=0)
-            result = right(image / blurred, wxb[v])
-            rpad[v, PAD + z] = result[:height]
-            rpad[v, PAD + z + 1] = result[height:]
-            return carry
-        lax.fori_loop(0, depth // 2, step, 0)
-
-    def start(group):
-        for c in group:
-            c.start()
-
-    for v in range(views):
-        ratio(v)
+    ratio(0, wyo[...], [(0, 3 * PAD), (yext - 3 * PAD, 3 * PAD)], [0, height - PAD], PAD)
+    start(r_outer[0])
+    for v in range(1, views):
+        y_bands(v)
+        x_bands(v)
+        whole(v)
+        sent(r_mid[0] if v == 1 else r_outer[v - 2])
         start(r_outer[v])
-        if v == 0:
-            start(r_mid[v])
-    for v in range(1, views):
-        start(r_mid[v])
+    y_bands(0)
 
     def correction(v, first, planes):
         covered = jnp.full((height, width), cov[v, 0, 0], jnp.int32) > 0
 
         def step(k, carry):
-            z = first + 2 * k
-            result = left(wyb[v], [cpad[v, z + j] for j in range(2)])
-            for j in range(2):
+            z = first + 4 * k
+            result = left(wyb[v], [cpad[v, z + j] for j in range(4)])
+            for j in range(4):
                 masked = jnp.where(covered, result[:, j * width:(j + 1) * width], jnp.float32(1.0))
                 acc[z + j] = masked if v == 0 else acc[z + j] * masked
             return carry
-        lax.fori_loop(0, planes // 2, step, 0)
+        lax.fori_loop(0, planes // 4, step, 0)
 
     def outer(v):
         for c in r_outer[v]:
@@ -268,19 +337,36 @@
     def mid(v):
         for c in r_mid[v]:
             c.wait_recv()
-        backward_z(v, PAD, height - 2 * PAD)
+        backward_z(v, PAD, inner)
+
+    def finish(v):
         for c in c_y[v]:
             c.wait_recv()
+        correction(v, 0, depth)
+
+    def begin(k):
+        pieces = [r_outer[views - 2], r_outer[views - 1]] + r_mid[1:] + r_last
+        sent(pieces[k])
+        start(pieces[k + 2])
 
     outer(0)
     mid(0)
-    correction(0, 0, depth)
+    begin(0)
+    finish(0)
     for v in range(1, views):
         outer(v)
+        if v == 1:
+            begin(1)
     for v in range(1, views - 1):
         mid(v)
-        correction(v, 0, depth)
-    mid(views - 1)
+        begin(v + 1)
+        finish(v)
+    for k in range(2):
+        for c in r_last[k]:
+            c.wait_recv()
+        backward_z(views - 1, PAD + k * inner // 2, inner // 2)
+    for c in c_y[views - 1]:
+        c.wait_recv()
 
     per = depth // PARTS
     exchange = []
@@ -301,16 +387,17 @@
             return carry
         lax.fori_loop(k * per, (k + 1) * per, step, 0)
 
-    for c in f_z + f_y:
+    for c in f_z[0] + f_z[1] + f_s[0] + f_s[1] + f_y:
         c.wait_send()
     for zs, _ in sides:
         @pl.when(has["gz", -zs])
         def _(zs=zs):
             for c in f_c[zs]:
                 c.wait_send()
+    for k in range(2):
+        sent(r_last[k])
     for v in range(views):
-        for c in r_outer[v] + r_mid[v] + c_y[v]:
-            c.wait_send()
+        sent(c_y[v])
     for part in exchange:
         part.wait_send()
 
@@ -344,6 +431,8 @@
                 pltpu.VMEM((views, 2 * depth, 2 * zext), bf16),
                 pltpu.VMEM((views, 2 * height, 2 * yext), bf16),
                 pltpu.VMEM((views, 2 * height, 2 * yext), bf16),
+                pltpu.VMEM((2 * (height - 2 * PAD), 2 * height), bf16),
+                pltpu.VMEM((2 * PAD, 6 * PAD), bf16),
                 pltpu.VMEM((views, 2 * width, 2 * width), bf16),
                 pltpu.VMEM((views, 2 * width, 2 * width), bf16),
                 pltpu.SemaphoreType.DMA((64,)),
@@ -351,7 +440,7 @@
                 pltpu.SemaphoreType.DMA((2,)),
             ],
             compiler_params=pltpu.CompilerParams(
-                collective_id=0, has_side_effects=True, vmem_limit_bytes=40 * 2**20),
+                collective_id=0, has_side_effects=True, vmem_limit_bytes=60 * 2**20),
         )(psf, coverage, images, estimate)
 
     return jax.shard_map(

time: 70.9 us -> 59.3 us (0.84)
  Pallas kernels: 66 us -> 55.9 us
  local copies, waits for them, and re-layouts: 4.68 us -> 3.18 us
    pallas_call x1, Pallas kernels: 66 us -> 55.9 us  [body(): pl.pallas_call(functools.partial(kernel, images.shape, zpeers, ypeers), o...]
    unnamed x8 -> x2, local copies, waits for them, and re-layouts: 4.68 us -> 3.18 us
where the time goes in v2:
time: 59.3 us; the launch traced here: 59.1 us
  Pallas kernels  55.9 us (94%)
  local copies, waits for them, and re-layouts  3.18 us (5%)
    pallas_call x1, Pallas kernels, body(): pl.pallas_call(functools.partial(kernel, images.shape, zpeers, ypeers), o...  55.9 us
    unnamed x2, local copies, waits for them, and re-layouts  3.18 us

profile of v2, /device:TPU:0, one launch (start us, length us, event | category | flops | bytes accessed | tf_op | source)
XLA Modules:
  0.0 59.1 jit_solution(13388090240557630751)
XLA Ops:
  0.0 1.3 %copy.5.cov = s32[3,1,1]{2,1,0:T(1,128)} copy(s32[3,1,1]{0,2,1:T(1,128)} %param.7) | data formatting | bytes 24 | tf_op args[3]
  1.3 55.9 %shard_map.46 = f32[16,64,128]{2,1,0:T(8,128)} custom-call(f32[3,3,31]{2,1,0:T(4,128)} %psf.1, s32[3,1,1]{2,1,0:T(1,128)} %copy.5.cov, f32[3,16,64,128]{3,2,1,0:T(8,128)} %images_hbm.1, f32[16,64,128]{2,1,0:T(8,128)} %est_hbm.1), custom_call_target="tpu_custom_call" | custom-call | tf_op jit(solution)/shard_map/pallas_call | solution.py:412
  57.2 1.9 %copy.7 = f32[16,64,128]{2,1,0:T(8,128)} copy(f32[16,64,128]{2,1,0:T(8,128)} %shard_map.46) | data formatting | bytes 1048576

commit v3 on v2

--- a/solution.py
+++ b/solution.py
@@ -241,28 +241,29 @@
 
     for v in range(views):
         z_bands(v)
+    part_bands()
+    x_bands(0)
     est_copy.wait()
     for k in range(2):
         for c, d in zip(f_z[k], f_s[k]):
             c.wait_recv()
             d.start()
+        for d in f_s[k]:
+            d.wait_recv()
         if k == 0:
-            part_bands()
-            for d in f_s[0]:
-                d.wait_recv()
             for zs, _ in sides:
                 @pl.when(has["gz", -zs])
                 def _(zs=zs):
                     for c in f_c[zs]:
                         c.start()
-            x_bands(0)
-    for d in f_s[1]:
-        d.wait_recv()
-    forward_z(PAD, height)
+            forward_z(PAD, quarter)
+            forward_z(PAD + height - quarter, quarter)
+        else:
+            forward_z(PAD + quarter, height - 2 * quarter)
     images_copy.wait()
 
     def ratio(v, weights, blocks, first, rows):
-        planes = 4
+        planes = 4 * height // (len(first) * rows)
 
         def step(k, carry):
             z = planes * k
@@ -316,7 +317,7 @@
     y_bands(0)
 
     def correction(v, first, planes):
-        covered = jnp.full((height, width), cov[v, 0, 0], jnp.int32) > 0
+        covered = jnp.full((height, width), cov[v], jnp.int32) > 0
 
         def step(k, carry):
             z = first + 4 * k
@@ -411,7 +412,7 @@
         f32, bf16 = jnp.float32, jnp.bfloat16
         return pl.pallas_call(
             functools.partial(kernel, images.shape, zpeers, ypeers),
-            out_shape=jax.ShapeDtypeStruct(estimate.shape, f32),
+            out_shape=pltpu.VMEM(estimate.shape, f32),
             in_specs=[
                 pl.BlockSpec(memory_space=pltpu.SMEM),
                 pl.BlockSpec(memory_space=pltpu.SMEM),
@@ -441,7 +442,7 @@
             ],
             compiler_params=pltpu.CompilerParams(
                 collective_id=0, has_side_effects=True, vmem_limit_bytes=60 * 2**20),
-        )(psf, coverage, images, estimate)
+        )(psf, coverage.reshape(views), images, estimate)
 
     return jax.shard_map(
         body,

time: 59.3 us -> 54.4 us (0.917)
  Pallas kernels: 55.9 us -> 53.4 us
  local copies, waits for them, and re-layouts: 3.18 us -> 0.8 us
    pallas_call x1, Pallas kernels: 55.9 us -> 53.4 us  [body(): pl.pallas_call(functools.partial(kernel, images.shape, zpeers, ypeers), o...]
    unnamed x2 -> x1, local copies, waits for them, and re-layouts: 3.18 us -> 0.8 us
where the time goes in v3:
time: 54.4 us; the launch traced here: 54.2 us
  Pallas kernels  53.4 us (98%)
  local copies, waits for them, and re-layouts  0.8 us (1%)
    pallas_call x1, Pallas kernels, body(): pl.pallas_call(functools.partial(kernel, images.shape, zpeers, ypeers), o...  53.4 us

profile of v3, /device:TPU:0, one launch (start us, length us, event | category | flops | bytes accessed | tf_op | source)
XLA Modules:
  0.0 54.2 jit_solution(17923213507239154911)
XLA Ops:
  0.0 53.4 %shard_map.46 = f32[16,64,128]{2,1,0:T(8,128)S(1)} custom-call(f32[3,3,31]{2,1,0:T(4,128)} %psf.1, s32[3]{0:T(128)} %bitcast.1, f32[3,16,64,128]{3,2,1,0:T(8,128)} %images_hbm.1, f32[16,64,128]{2,1,0:T(8,128)} %est_hbm.1), custom_call_target="tpu_custom_call" | custom-call | tf_op jit(solution)/shard_map/pallas_call | solution.py:413
  53.4 0.8 %copy.6 = f32[16,64,128]{2,1,0:T(8,128)} copy(f32[16,64,128]{2,1,0:T(8,128)S(1)} %shard_map.46) | data formatting | bytes 1048576

commit v4 on v3

--- a/solution.py
+++ b/solution.py
@@ -282,7 +282,7 @@
                     rpad[v, PAD + z + j, pl.ds(f, rows), :] = result[at:at + rows]
                     at += rows
             return carry
-        lax.fori_loop(0, depth // planes, step, 0)
+        lax.fori_loop(0, depth // planes, step, 0, unroll=2)
 
     def start(group):
         for c in group:

time: 54.4 us -> 54.2 us (level)
  no operation moved by 1% of the time
where the time goes in v4:
time: 54.2 us; the launch traced here: 54 us
  Pallas kernels  53.2 us (98%)
  local copies, waits for them, and re-layouts  0.8 us (1%)
    pallas_call x1, Pallas kernels, body(): pl.pallas_call(functools.partial(kernel, images.shape, zpeers, ypeers), o...  53.2 us

profile of v4, /device:TPU:0, one launch (start us, length us, event | category | flops | bytes accessed | tf_op | source)
XLA Modules:
  0.0 54.0 jit_solution(17415975290576303530)
XLA Ops:
  0.0 53.2 %shard_map.46 = f32[16,64,128]{2,1,0:T(8,128)S(1)} custom-call(f32[3,3,31]{2,1,0:T(4,128)} %psf.1, s32[3]{0:T(128)} %bitcast.1, f32[3,16,64,128]{3,2,1,0:T(8,128)} %images_hbm.1, f32[16,64,128]{2,1,0:T(8,128)} %est_hbm.1), custom_call_target="tpu_custom_call" | custom-call | tf_op jit(solution)/shard_map/pallas_call | solution.py:413
  53.2 0.8 %copy.6 = f32[16,64,128]{2,1,0:T(8,128)} copy(f32[16,64,128]{2,1,0:T(8,128)S(1)} %shard_map.46) | data formatting | bytes 1048576
